TPU v7x, 256 devices: a whole 4x4x8 slice. The times are simulated.
256 devices in a mesh: ctx: 32 (over y, z), head: 8 (over x, core).
Axes of the slice: x: 4, y: 4, z: 8, core: 2. Of those that a mesh axis runs over, the one named last changes fastest.
Arguments:
- query: bfloat16 [32768, 5120], P('ctx', 'head'), may hold values from -800 to 800
- key: bfloat16 [32768, 5120], P('ctx', 'head'), may hold values from -800 to 800
- value: bfloat16 [32768, 5120], P('ctx', 'head'), may hold values from -6 to 6
- gain_q: float32 [5120], P('head'), may hold values from 0.1 to 1.9
- gain_k: float32 [5120], P('head'), may hold values from 0.1 to 1.9
- head_kind: int32 [40], replicated, may hold values from 0 to 1, as said below
Outputs:
- attended: bfloat16 [32768, 5120], P('ctx', 'head')
Inputs may be any that keep to these rules, and one draw needn't show every extreme that they name: `head_kind`: 1 marks a temporal head, 0 a spatial one; each aligned group of 5 heads (heads 0 to 4, and so on) holds 1 to 3 temporal heads, and in every draw some group holds exactly 1 and some exactly 3.
All inputs are finite; a program needn't handle non-finite values.
Results may differ from a plain program's by a relative error of at most 0.012.
Values may be sent and summed in bfloat16 or wider, within the bound.
A program may use at most 64 MiB of HBM per device.

v0:
```python
import math

import jax
import jax.numpy as jnp
from jax import lax
from jax.sharding import PartitionSpec as P

HEADS = 40
HDIM = 128


EPSILON = 1e-06


def partner(shard, axis, distance):
    return lax.ppermute(shard, axis, [(i, i ^ 1 << distance) for i in range(lax.axis_size(axis))])


def softmax_weights(scores):
    row_top = jnp.max(scores, axis=-1, keepdims=True)
    expo_terms = jnp.exp(scores - row_top)
    return (expo_terms / jnp.sum(expo_terms, axis=-1, keepdims=True)).astype(jnp.bfloat16)


def shards(query, key, value, gain_q, gain_k, head_kind):
    positions, row_width = query.shape
    heads_dev = row_width // HDIM
    frame_total = lax.axis_size("ctx") // 2
    score_scale = 1.0 / math.sqrt(HDIM)
    query_float = query.astype(jnp.float32)
    key_float = key.astype(jnp.float32)
    query_total, key_total = lax.psum(
        (jnp.sum(query_float * query_float, axis=1), jnp.sum(key_float * key_float, axis=1)), "head"
    )
    query_norm = (
        query_float * lax.rsqrt(query_total / (HEADS * HDIM) + EPSILON)[:, None] * gain_q
    ).astype(jnp.bfloat16)
    key_norm = (
        key_float * lax.rsqrt(key_total / (HEADS * HDIM) + EPSILON)[:, None] * gain_k
    ).astype(jnp.bfloat16)
    partner_key, partner_value = partner((key_norm, value), "ctx", 0)
    key_frame = jnp.concatenate([key_norm, partner_key], axis=0)
    value_frame = jnp.concatenate([value, partner_value], axis=0)
    local_kind = lax.dynamic_slice_in_dim(head_kind, lax.axis_index("head") * heads_dev, heads_dev)

    def spatial_head(head_index):
        query_head = lax.dynamic_slice_in_dim(query_norm, head_index * HDIM, HDIM, 1)
        key_head = lax.dynamic_slice_in_dim(key_frame, head_index * HDIM, HDIM, 1)
        value_head = lax.dynamic_slice_in_dim(value_frame, head_index * HDIM, HDIM, 1)
        scores = (
            jnp.einsum("pd,sd->ps", query_head, key_head, preferred_element_type=jnp.float32)
            * score_scale
        )
        weights = softmax_weights(scores)
        return jnp.einsum(
            "ps,sd->pd", weights, value_head, preferred_element_type=jnp.float32
        ).astype(jnp.bfloat16)

    spatial = lax.map(spatial_head, jnp.arange(heads_dev, dtype=jnp.int32))
    query_three = query_norm.reshape(positions, heads_dev, HDIM)
    key_three = key_norm.reshape(positions, heads_dev, HDIM)
    value_three = value.reshape(positions, heads_dev, HDIM)
    outgoing = (query_three[None], key_three[None], value_three[None])
    query_part = lax.all_to_all(outgoing[0], "ctx", split_axis=1, concat_axis=0, tiled=True)
    key_part = lax.all_to_all(outgoing[1], "ctx", split_axis=1, concat_axis=0, tiled=True)
    value_part = lax.all_to_all(outgoing[2], "ctx", split_axis=1, concat_axis=0, tiled=True)
    sources, rows, items, depth = query_part.shape
    query_five = query_part.reshape(frame_total, 2, rows, items, depth)
    key_five = key_part.reshape(frame_total, 2, rows, items, depth)
    value_five = value_part.reshape(frame_total, 2, rows, items, depth)
    scores = (
        jnp.einsum("fhpnd,ghpnd->hpnfg", query_five, key_five, preferred_element_type=jnp.float32)
        * score_scale
    )
    weights = softmax_weights(scores)
    mixed_out = jnp.einsum(
        "hpnfg,ghpnd->fhpnd", weights, value_five, preferred_element_type=jnp.float32
    ).astype(jnp.bfloat16)
    mixed_out = mixed_out.reshape(sources, rows, items, depth)
    arrived = lax.all_to_all(mixed_out, "ctx", split_axis=0, concat_axis=1, tiled=True)[0]
    temporal_mask = (local_kind == 1)[None, :, None]
    result = jnp.where(temporal_mask, arrived, jnp.transpose(spatial, (1, 0, 2)))
    return result.reshape(positions, row_width)


def solution(mesh):
    return jax.shard_map(
        shards,
        mesh=mesh,
        in_specs=(P("ctx", "head"), P("ctx", "head"), P("ctx", "head"), P("head"), P("head"), P()),
        out_specs=P("ctx", "head"),
        check_vma=False,
    )
```

profile of v0, /device:TPU:1, one launch (start us, length us, event | category | flops | bytes accessed | tf_op | source)
XLA Modules:
  0.0 310.2 jit_solution(11390492724262679645)
XLA Ops:
  1.6 2.1 copy.43
  4.4 15.2 %all-reduce = (f32[1024]{0:T(1024)S(1)}, f32[1024]{0:T(1024)S(1)}) all-reduce(f32[1024]{0:T(1024)S(1)} %get-tuple-element.74, f32[1024]{0:T(1024)S(1)} %get-tuple-element.75), channel_id=1, replica_groups=mesh['ctx'=32,'head'=8] {'head'}, use_global_device_ids=true, to_apply=%region_1.0 | all-reduce | flops 2048 | bytes 16384 | tf_op jit(solution)/shard_map/psum | solution.py:32
  21.3 2.8 copy.44
  24.1 9.7 %all-to-all-start.1 = ((bf16[1,1024,5,128]{3,2,0,1:T(8,128)(2,1)}), bf16[1,1024,5,128]{3,2,0,1:T(8,128)(2,1)}, u32[]{:S(2)}, u32[]{:S(2)}) async-start(bf16[1,1024,5,128]{3,2,0,1:T(8,128)(2,1)} %copy.44), calls=%async_computation.1 | async-start | bytes 4194304 | tf_op jit(solution)/shard_map/all_to_all | solution.py:65
  35.5 2.8 copy.41
  38.3 43.6 %all-to-all-done.1 = bf16[1,1024,5,128]{3,2,0,1:T(8,128)(2,1)} async-done(((bf16[1,1024,5,128]{3,2,0,1:T(8,128)(2,1)}), bf16[1,1024,5,128]{3,2,0,1:T(8,128)(2,1)}, u32[]{:S(2)}, u32[]{:S(2)}) %all-to-all-start.1) | async-done | bytes 1310752 | tf_op jit(solution)/shard_map/all_to_all | solution.py:65
  81.9 6.1 %all-to-all-start = ((bf16[1,1024,5,128]{3,2,0,1:T(8,128)(2,1)}), bf16[1,1024,5,128]{3,2,0,1:T(8,128)(2,1)}, u32[]{:S(2)}, u32[]{:S(2)}) async-start(bf16[1,1024,5,128]{3,2,0,1:T(8,128)(2,1)} %copy.41), calls=%async_computation | async-start | bytes 4194304 | tf_op jit(solution)/shard_map/all_to_all | solution.py:64
  89.3 2.4 copy.48
  91.7 3.9 %copy.49 = bf16[1,1024,5,128]{3,2,0,1:T(8,128)(2,1)} copy(bf16[1,1024,5,128]{1,3,2,0:T(8,128)(2,1)} %bitcast.27) | data formatting | bytes 2621440 | tf_op jit(solution)/shard_map/broadcast_in_dim;reshape | solution.py:63
  95.6 40.6 %all-to-all-done = bf16[1,1024,5,128]{3,2,0,1:T(8,128)(2,1)} async-done(((bf16[1,1024,5,128]{3,2,0,1:T(8,128)(2,1)}), bf16[1,1024,5,128]{3,2,0,1:T(8,128)(2,1)}, u32[]{:S(2)}, u32[]{:S(2)}) %all-to-all-start) | async-done | bytes 1310752 | tf_op jit(solution)/shard_map/all_to_all | solution.py:64
  136.2 5.8 %all-to-all-start.2 = ((bf16[1,1024,5,128]{3,2,0,1:T(8,128)(2,1)}), bf16[1,1024,5,128]{3,2,0,1:T(8,128)(2,1)}, u32[]{:S(2)}, u32[]{:S(2)}) async-start(bf16[1,1024,5,128]{3,2,0,1:T(8,128)(2,1)} %copy.49), calls=%async_computation.2 | async-start | bytes 4194304 | tf_op jit(solution)/shard_map/all_to_all | solution.py:66
  143.3 29.7 %collective-permute-done = bf16[1024,640]{0,1:T(8,128)(2,1)} collective-permute-done((bf16[1024,640]{0,1:T(8,128)(2,1)S(1)}, bf16[1024,640]{0,1:T(8,128)(2,1)}, u32[]{:S(2)}, u32[]{:S(2)}) %collective-permute-start) | collective-permute-done | bytes 1310752 | tf_op jit(solution)/shard_map/ppermute | solution.py:16
  173.0 3.1 %pad_maximum_fusion = bf16[2048,640]{0,1:T(8,128)(2,1)} fusion(bf16[1024,640]{0,1:T(8,128)(2,1)} %collective-permute-done, bf16[1024,640]{0,1:T(8,128)(2,1)S(1)} %fusion.18), kind=kLoop, calls=%fused_computation.26 | loop fusion | flops 5242880 | bytes 5242880 | tf_op jit(solution)/shard_map/concatenate | solution.py:42
  176.1 58.7 %collective-permute-done.1 = bf16[1024,640]{1,0:T(8,128)(2,1)} collective-permute-done((bf16[1024,640]{1,0:T(8,128)(2,1)}, bf16[1024,640]{1,0:T(8,128)(2,1)}, u32[]{:S(2)}, u32[]{:S(2)}) %collective-permute-start.1) | collective-permute-done | bytes 1310752 | tf_op jit(solution)/shard_map/ppermute | solution.py:16
  234.8 3.1 pad_maximum_fusion.1
  237.9 4.1 %fusion.24 = f32[2,32,5,16,16]{3,4,2,1,0:T(8,128)S(1)} fusion(bf16[16,2,32,5,128]{4,3,2,1,0:T(8,128)(2,1)} %bitcast.5, bf16[16,2,32,5,128]{4,3,2,1,0:T(8,128)(2,1)} %bitcast.3), kind=kOutput, calls=%fused_computation.36 | convolution fusion | flops 20971520 | bytes 2949120 | tf_op jit(solution)/shard_map/fhpnd,ghpnd->hpnfg/dot_general | solution.py:72
  242.0 2.5 fusion.30
  244.4 3.6 %fusion.22 = bf16[16,2,32,5,128]{4,0,3,2,1:T(8,128)(2,1)S(1)} fusion(f32[2,32,5,16,16]{3,4,2,1,0:T(8,128)} %get-tuple-element.73, bf16[16,2,32,5,128]{4,3,2,1,0:T(8,128)(2,1)} %bitcast.7, f32[2,32,5,16]{3,2,1,0:T(8,128)S(1)} %get-tuple-element.72), kind=kOutput, calls=%fused_computation.33 | convolution fusion | flops 21790720 | bytes 2969600 | tf_op jit(solution)/shard_map/hpnfg,ghpnd->fhpnd/dot_general | solution.py:76
  249.5 9.2 %all-to-all-start.3 = ((bf16[32,32,5,128]{3,1,2,0:T(8,128)(2,1)}), bf16[32,32,5,128]{3,1,2,0:T(8,128)(2,1)S(1)}, u32[]{:S(2)}, u32[]{:S(2)}) async-start(bf16[32,32,5,128]{3,1,2,0:T(8,128)(2,1)} %bitcast.25), calls=%async_computation.3 | async-start | bytes 2621440 | tf_op jit(solution)/shard_map/all_to_all | solution.py:80
  258.7 47.7 %while.10 = (s32[]{:T(128)}, bf16[5,1024,128]{2,1,0:T(8,128)(2,1)}, s32[5]{0:T(128)S(1)}, bf16[1024,640]{0,1:T(8,128)(2,1)S(1)}, bf16[2048,640]{0,1:T(8,128)(2,1...) while((s32[]{:T(128)}, bf16[5,1024,128]{2,1,0:T(8,128)(2,1)}, ...), condition=%wide.region_9.10_spmd, body=%wide.region_6.9_spmd.sunk | while | flops 1092745216 | bytes 26760868 | solution.py:59
  260.0 2.4 multiply_reduce_fusion.3
  262.4 1.9 fusion.35
  264.3 3.9 %fusion.36 = bf16[5,1024,128]{2,1,0:T(8,128)(2,1)} fusion(bf16[5,1024,128]{2,1,0:T(8,128)(2,1)} %get-tuple-element.128, s32[]{:T(128)} %get-tuple-element.127, f32[1024,2048]{1,0:T(8,128)S(1)} %get-tuple-element.115, f32[1024]{0:T(1024)S(1)} %fusion.35, f32[1024]{0:T(1024)S(1)} %get-tuple-element.116, bf16[2048,640]{1,0:T(8,128)(2,1)} %get-tuple-element.142, ...), kind=kOutput, calls=%fused_computation.7.clone.1 | convolution fusion | flops 545390592 | bytes 9183748 | tf_op jit(solution)/shard_map/while/body/eval_jaxpr/ps,sd->pd/dot_general | solution.py:55
  269.5 2.4 multiply_reduce_fusion.3
  271.9 1.9 fusion.35
  273.9 3.9 %fusion.36 = bf16[5,1024,128]{2,1,0:T(8,128)(2,1)} fusion(bf16[5,1024,128]{2,1,0:T(8,128)(2,1)} %get-tuple-element.128, s32[]{:T(128)} %get-tuple-element.127, f32[1024,2048]{1,0:T(8,128)S(1)} %get-tuple-element.115, f32[1024]{0:T(1024)S(1)} %fusion.35, f32[1024]{0:T(1024)S(1)} %get-tuple-element.116, bf16[2048,640]{1,0:T(8,128)(2,1)} %get-tuple-element.142, ...), kind=kOutput, calls=%fused_computation.7.clone.1 | convolution fusion | flops 545390592 | bytes 9183748 | tf_op jit(solution)/shard_map/while/body/eval_jaxpr/ps,sd->pd/dot_general | solution.py:55
  279.0 2.4 multiply_reduce_fusion.3
  283.4 3.9 %fusion.36 = bf16[5,1024,128]{2,1,0:T(8,128)(2,1)} fusion(bf16[5,1024,128]{2,1,0:T(8,128)(2,1)} %get-tuple-element.128, s32[]{:T(128)} %get-tuple-element.127, f32[1024,2048]{1,0:T(8,128)S(1)} %get-tuple-element.115, f32[1024]{0:T(1024)S(1)} %fusion.35, f32[1024]{0:T(1024)S(1)} %get-tuple-element.116, bf16[2048,640]{1,0:T(8,128)(2,1)} %get-tuple-element.142, ...), kind=kOutput, calls=%fused_computation.7.clone.1 | convolution fusion | flops 545390592 | bytes 9183748 | tf_op jit(solution)/shard_map/while/body/eval_jaxpr/ps,sd->pd/dot_general | solution.py:55
  288.6 2.4 multiply_reduce_fusion.3
  292.9 3.9 %fusion.36 = bf16[5,1024,128]{2,1,0:T(8,128)(2,1)} fusion(bf16[5,1024,128]{2,1,0:T(8,128)(2,1)} %get-tuple-element.128, s32[]{:T(128)} %get-tuple-element.127, f32[1024,2048]{1,0:T(8,128)S(1)} %get-tuple-element.115, f32[1024]{0:T(1024)S(1)} %fusion.35, f32[1024]{0:T(1024)S(1)} %get-tuple-element.116, bf16[2048,640]{1,0:T(8,128)(2,1)} %get-tuple-element.142, ...), kind=kOutput, calls=%fused_computation.7.clone.1 | convolution fusion | flops 545390592 | bytes 9183748 | tf_op jit(solution)/shard_map/while/body/eval_jaxpr/ps,sd->pd/dot_general | solution.py:55
  298.1 2.4 multiply_reduce_fusion.3
  302.4 3.9 %fusion.36 = bf16[5,1024,128]{2,1,0:T(8,128)(2,1)} fusion(bf16[5,1024,128]{2,1,0:T(8,128)(2,1)} %get-tuple-element.128, s32[]{:T(128)} %get-tuple-element.127, f32[1024,2048]{1,0:T(8,128)S(1)} %get-tuple-element.115, f32[1024]{0:T(1024)S(1)} %fusion.35, f32[1024]{0:T(1024)S(1)} %get-tuple-element.116, bf16[2048,640]{1,0:T(8,128)(2,1)} %get-tuple-element.142, ...), kind=kOutput, calls=%fused_computation.7.clone.1 | convolution fusion | flops 545390592 | bytes 9183748 | tf_op jit(solution)/shard_map/while/body/eval_jaxpr/ps,sd->pd/dot_general | solution.py:55
  (38 shorter events, 22.4 us)
Async XLA Ops:
  1.6 2.7 copy-start
  1.6 18.0 %copy-start.3 = (f32[640]{0:T(1024)S(1)}, f32[640]{0:T(1024)}, u32[]{:S(2)}) copy-start(f32[640]{0:T(1024)} %param.12) | copy-start | bytes 7684
  3.7 15.9 %copy-start.1 = (bf16[1024,640]{0,1:T(8,128)(2,1)}, bf16[1024,640]{0,1:T(8,128)(2,1)S(1)}, u32[]{:S(2)}) copy-start(bf16[1024,640]{0,1:T(8,128)(2,1)S(1)} %copy.43) | copy-start | bytes 3932164
  24.1 9.8 %copy-start.4 = (f32[640]{0:T(1024)S(1)}, f32[640]{0:T(1024)}, u32[]{:S(2)}) copy-start(f32[640]{0:T(1024)} %param.11) | copy-start | bytes 7684
  24.1 57.8 %all-to-all-start.1 = ((bf16[1,1024,5,128]{3,2,0,1:T(8,128)(2,1)}), bf16[1,1024,5,128]{3,2,0,1:T(8,128)(2,1)}, u32[]{:S(2)}, u32[]{:S(2)}) async-start(bf16[1,1024,5,128]{3,2,0,1:T(8,128)(2,1)} %copy.44), calls=%async_computation.1 | async-start | bytes 4194304 | tf_op jit(solution)/shard_map/all_to_all | solution.py:65
  81.9 54.3 %all-to-all-start = ((bf16[1,1024,5,128]{3,2,0,1:T(8,128)(2,1)}), bf16[1,1024,5,128]{3,2,0,1:T(8,128)(2,1)}, u32[]{:S(2)}, u32[]{:S(2)}) async-start(bf16[1,1024,5,128]{3,2,0,1:T(8,128)(2,1)} %copy.41), calls=%async_computation | async-start | bytes 4194304 | tf_op jit(solution)/shard_map/all_to_all | solution.py:64
  88.0 85.0 %collective-permute-start = (bf16[1024,640]{0,1:T(8,128)(2,1)S(1)}, bf16[1024,640]{0,1:T(8,128)(2,1)}, u32[]{:S(2)}, u32[]{:S(2)}) collective-permute-start(bf16[1024,640]{0,1:T(8,128)(2,1)S(1)} %fusion.18), channel_id=1, source_target_pairs={{0,8},{8,0},{16,24},{24,16},{32,40},{40,32},{48,56},{56,48},{64,72... | collective-permute-start | bytes 3932168 | tf_op jit(solution)/shard_map/ppermute | solution.py:16
  95.6 47.6 %copy-start.5 = (s32[40]{0:T(128)S(1)}, s32[40]{0:T(128)}, u32[]{:S(2)}) copy-start(s32[40]{0:T(128)} %param.13) | copy-start | bytes 484
  136.2 108.3 %all-to-all-start.2 = ((bf16[1,1024,5,128]{3,2,0,1:T(8,128)(2,1)}), bf16[1,1024,5,128]{3,2,0,1:T(8,128)(2,1)}, u32[]{:S(2)}, u32[]{:S(2)}) async-start(bf16[1,1024,5,128]{3,2,0,1:T(8,128)(2,1)} %copy.49), calls=%async_computation.2 | async-start | bytes 4194304 | tf_op jit(solution)/shard_map/all_to_all | solution.py:66
  142.0 92.8 %collective-permute-start.1 = (bf16[1024,640]{1,0:T(8,128)(2,1)}, bf16[1024,640]{1,0:T(8,128)(2,1)}, u32[]{:S(2)}, u32[]{:S(2)}) collective-permute-start(bf16[1024,640]{1,0:T(8,128)(2,1)} %param.10), channel_id=1, source_target_pairs={{0,8},{8,0},{16,24},{24,16},{32,40},{40,32},{48,56},{56,48},{64,72... | collective-permute-start | bytes 3932168 | tf_op jit(solution)/shard_map/ppermute | solution.py:16
  143.3 91.5 %copy-start.2 = (bf16[1024,640]{1,0:T(8,128)(2,1)S(1)}, bf16[1024,640]{1,0:T(8,128)(2,1)}, u32[]{:S(2)}) copy-start(bf16[1024,640]{1,0:T(8,128)(2,1)} %param.10) | copy-start | bytes 3932164
  249.5 56.9 %all-to-all-start.3 = ((bf16[32,32,5,128]{3,1,2,0:T(8,128)(2,1)}), bf16[32,32,5,128]{3,1,2,0:T(8,128)(2,1)S(1)}, u32[]{:S(2)}, u32[]{:S(2)}) async-start(bf16[32,32,5,128]{3,1,2,0:T(8,128)(2,1)} %bitcast.25), calls=%async_computation.3 | async-start | bytes 2621440 | tf_op jit(solution)/shard_map/all_to_all | solution.py:80
where the time goes:
time: 315 us; the launch traced here: 310 us
  waiting for transfers between devices  173 us (55%)
  matrix products  39.3 us (12%)
  starting transfers between devices  33.3 us (11%)
  other arithmetic  23.8 us (8%)
  local copies, waits for them, and re-layouts  22.7 us (7%)
  blocking collectives  15.2 us (5%)
  loops' own time  3.18 us (1%)
    ppermute x2, waiting for transfers between devices, partner(): lax.ppermute(shard, axis, [(i, i ^ 1 << distance) for i in range(lax.axis...  88.3 us
    all_to_all x1, waiting for transfers between devices, shards(): lax.all_to_all(outgoing[1], 'ctx', split_axis=1, concat_axis=0, tiled=True)  43.6 us
    all_to_all x1, waiting for transfers between devices, shards(): lax.all_to_all(outgoing[0], 'ctx', split_axis=1, concat_axis=0, tiled=True)  40.6 us
    dot_general x5, matrix products, spatial_head(): jnp.einsum('ps,sd->pd', weights, value_head, preferred_element_type=jnp.f...  19.6 us
    psum x1, blocking collectives, shards(): lax.psum((jnp.sum(query_float * query_float, axis=1), jnp.sum(key_float *...  15.2 us
    dot_general x5, matrix products, spatial_head(): jnp.einsum('pd,sd->ps', query_head, key_head, preferred_element_type=jnp....  12 us
    all_to_all x1, starting transfers between devices, shards(): lax.all_to_all(outgoing[1], 'ctx', split_axis=1, concat_axis=0, tiled=True)  9.73 us
    reduce_sum x5, other arithmetic, softmax_weights(): jnp.sum(expo_terms, axis=-1, keepdims=True)  9.67 us
  transfers between devices with their start and end apart: 6, of which 4 were waited for; matrix products, arithmetic and copies ran while one was open for 22% of the time, Pallas kernels for 0%

commit v1 on v0

v1 whole, which is shorter than its diff:
```python
import functools
import math

import jax
import jax.numpy as jnp
from jax import lax
from jax.experimental import pallas as pl
from jax.experimental.pallas import tpu as pltpu
from jax.sharding import PartitionSpec as P

HEADS = 40
HDIM = 128
EPSILON = 1e-06
NT = 3
NS = 4
CHUNK = 128
QROWS = 256
MESH = pl.DeviceIdType.MESH
BF16 = jnp.bfloat16
F32 = jnp.float32


def dot_nt(a, b):
    return lax.dot_general(a, b, (((1,), (1,)), ((), ())), preferred_element_type=F32)


def dot_nn(a, b):
    return lax.dot_general(a, b, (((1,), (0,)), ((), ())), preferred_element_type=F32)


def kernel(
    frames, groups, kind_ref, q_ref, k_ref, v_ref, gq_ref, gk_ref, out_ref,
    vt, qkt, vr, qkr, ot, res, own_k, own_v, par_k, par_v, qs, qn, kn, rq, rk, ss_own, ss_all,
    ss_sems, vt_send, vt_recv, qk_send, qk_recv, ret_send, ret_recv,
    sk_send, sk_recv, sv_send, sv_recv,
):
    tokens, width = q_ref.shape
    heads = width // HDIM
    block = tokens // frames
    chunks = tokens // CHUNK
    score_scale = 1.0 / math.sqrt(HDIM)
    ctx = lax.axis_index("ctx")
    group = lax.axis_index("head")
    frame, half = ctx // 2, ctx % 2
    partner = ctx + 1 - 2 * half

    barrier = pltpu.get_barrier_semaphore()

    def peer_of(d):
        return lax.rem(frame + d, frames)

    def greet_ctx(d, carry):
        pl.semaphore_signal(
            barrier, inc=1, device_id={"ctx": 2 * peer_of(d) + half}, device_id_type=MESH
        )
        return carry

    def greet_head(d, carry):
        pl.semaphore_signal(
            barrier, inc=1, device_id={"head": lax.rem(group + d, groups)}, device_id_type=MESH
        )
        return carry

    pl.semaphore_signal(barrier, inc=1, device_id={"ctx": partner}, device_id_type=MESH)
    lax.fori_loop(1, frames, greet_ctx, 0)
    lax.fori_loop(1, groups, greet_head, 0)

    one_hot = {}
    seen = jnp.zeros((1, HDIM), jnp.int32)
    for h in range(heads):
        kind = jnp.full((1, HDIM), kind_ref[group * heads + h], jnp.int32)
        for slot in range(NT + NS):
            if slot < NT:
                chosen = (kind == 1) & (seen == slot)
            else:
                chosen = (kind == 0) & (h - seen == slot - NT)
            one_hot[slot, h] = jnp.where(chosen, 1.0, 0.0).astype(BF16)
        seen = seen + kind

    def fits(slot, h):
        if slot < NT:
            return h >= slot
        return 0 <= h - (slot - NT) <= NT

    def pick(ref, slot):
        total = None
        for h in range(heads):
            if fits(slot, h):
                term = ref[:, h * HDIM : (h + 1) * HDIM] * one_hot[slot, h]
                total = term if total is None else total + term
        return total

    for j in range(NT):
        vt[j] = pick(v_ref, j).reshape(frames, block, HDIM)

    pl.semaphore_wait(barrier, frames - 1 + groups - 1 + 1)

    def send_v(j):
        def step(d, carry):
            to = peer_of(d)
            pltpu.make_async_remote_copy(
                src_ref=vt.at[j, to], dst_ref=vr.at[j, frame],
                send_sem=vt_send.at[j], recv_sem=vt_recv.at[j],
                device_id={"ctx": 2 * to + half}, device_id_type=MESH,
            ).start()
            return carry
        lax.fori_loop(1, frames, step, 0)

    def send_qk(j):
        def step(d, carry):
            to = peer_of(d)
            pltpu.make_async_remote_copy(
                src_ref=qkt.at[j, :, to], dst_ref=qkr.at[j, :, frame],
                send_sem=qk_send.at[j], recv_sem=qk_recv.at[j],
                device_id={"ctx": 2 * to + half}, device_id_type=MESH,
            ).start()
            return carry
        lax.fori_loop(1, frames, step, 0)

    def send_ret(j):
        def step(d, carry):
            to = peer_of(d)
            pltpu.make_async_remote_copy(
                src_ref=ot.at[j, to], dst_ref=res.at[j, frame],
                send_sem=ret_send.at[j], recv_sem=ret_recv.at[j],
                device_id={"ctx": 2 * to + half}, device_id_type=MESH,
            ).start()
            return carry
        lax.fori_loop(1, frames, step, 0)

    def pair_copy(src, dst, send, recv, j):
        return pltpu.make_async_remote_copy(
            src_ref=src.at[j], dst_ref=dst.at[j], send_sem=send.at[j], recv_sem=recv.at[j],
            device_id={"ctx": partner}, device_id_type=MESH,
        )

    def wait_bytes(ref, sem):
        pltpu.make_async_copy(ref, ref, sem).wait()

    for j in range(NT):
        send_v(j)

    sub = lax.broadcasted_iota(jnp.int32, (8, CHUNK), 0)

    def squares(i, carry):
        rows = pl.ds(pl.multiple_of(i * CHUNK, CHUNK), CHUNK)
        kept = []
        for ref, tile in ((q_ref, carry[0]), (k_ref, carry[1])):
            part = ref[rows, :].astype(F32)
            total = jnp.sum(part * part, axis=1, keepdims=True)
            row = jnp.broadcast_to(total, (CHUNK, CHUNK)).T[0:8]
            kept.append(jnp.where(sub == i, row, tile))
        return tuple(kept)

    zero = jnp.zeros((8, CHUNK), F32)
    tiles = lax.fori_loop(0, chunks, squares, (zero, zero))
    for n in range(2):
        ss_own[n] = tiles[n]
        ss_all[group, n] = tiles[n]

    def send_squares(d, carry):
        pltpu.make_async_remote_copy(
            src_ref=ss_own, dst_ref=ss_all.at[group],
            send_sem=ss_sems.at[0], recv_sem=ss_sems.at[1],
            device_id={"head": lax.rem(group + d, groups)}, device_id_type=MESH,
        ).start()
        return carry

    lax.fori_loop(1, groups, send_squares, 0)

    for j in range(NS):
        own_v[j] = pick(v_ref, NT + j)

    wait_bytes(ss_all.at[pl.ds(0, groups - 1)], ss_sems.at[1])
    for n, column in ((0, rq), (1, rk)):
        total = ss_all[0, n]
        for g in range(1, groups):
            total = total + ss_all[g, n]
        inverse = lax.rsqrt(total * (1.0 / (HEADS * HDIM)) + EPSILON)
        for i in range(chunks):
            column[pl.ds(i * CHUNK, CHUNK), :] = jnp.broadcast_to(
                inverse[i : i + 1, :], (CHUNK, CHUNK)
            ).T

    for h in range(heads):
        at = slice(h * HDIM, (h + 1) * HDIM)
        qn[:, at] = (q_ref[:, at].astype(F32) * rq[...] * gq_ref[:, at]).astype(BF16)
        kn[:, at] = (k_ref[:, at].astype(F32) * rk[...] * gk_ref[:, at]).astype(BF16)

    for j in range(NT):
        qkt[j, 0] = pick(qn, j).reshape(frames, block, HDIM)
        qkt[j, 1] = pick(kn, j).reshape(frames, block, HDIM)
        send_qk(j)
        vr[j, frame] = vt[j, frame]
        for n in range(2):
            qkr[j, n, frame] = qkt[j, n, frame]

    for j in range(NS):
        own_k[j] = pick(kn, NT + j)
        pair_copy(own_k, par_k, sk_send, sk_recv, j).start()
        pair_copy(own_v, par_v, sv_send, sv_recv, j).start()
        qs[j] = pick(qn, NT + j)

    step_rows = 16 * frames
    same = (
        lax.rem(lax.broadcasted_iota(jnp.int32, (step_rows, step_rows), 0), 16)
        == lax.rem(lax.broadcasted_iota(jnp.int32, (step_rows, step_rows), 1), 16)
    )
    for j in range(NT):
        wait_bytes(vr.at[j, pl.ds(0, frames - 1)], vt_recv.at[j])
        wait_bytes(qkr.at[j, :, pl.ds(0, frames - 1)], qk_recv.at[j])
        for c in range(block // 16):
            at = pl.ds(c * 16, 16)
            query = qkr[j, 0, :, at, :].reshape(step_rows, HDIM)
            key = qkr[j, 1, :, at, :].reshape(step_rows, HDIM)
            value = vr[j, :, at, :].reshape(step_rows, HDIM)
            scores = jnp.where(same, dot_nt(query, key) * score_scale, -jnp.inf)
            expo = jnp.exp(scores - jnp.max(scores, axis=1, keepdims=True))
            weights = (expo / jnp.sum(expo, axis=1, keepdims=True)).astype(BF16)
            mixed = dot_nn(weights, value).astype(BF16)
            ot[j, :, at, :] = mixed.reshape(frames, 16, HDIM)
        send_ret(j)
        res[j, frame] = ot[j, frame]

    def spatial(j, carry):
        pair_copy(own_k, par_k, sk_send, sk_recv, j).wait_recv()
        pair_copy(own_v, par_v, sv_send, sv_recv, j).wait_recv()
        own_key, own_value, par_key, par_value = own_k[j], own_v[j], par_k[j], par_v[j]

        def rows_step(i, inner):
            query = qs[j, pl.ds(pl.multiple_of(i * QROWS, QROWS), QROWS), :]
            s_own = dot_nt(query, own_key) * score_scale
            s_par = dot_nt(query, par_key) * score_scale
            top = jnp.maximum(
                jnp.max(s_own, axis=1, keepdims=True), jnp.max(s_par, axis=1, keepdims=True)
            )
            e_own = jnp.exp(s_own - top)
            e_par = jnp.exp(s_par - top)
            total = jnp.sum(e_own, axis=1, keepdims=True) + jnp.sum(e_par, axis=1, keepdims=True)
            mixed = dot_nn(e_own.astype(BF16), own_value) + dot_nn(e_par.astype(BF16), par_value)
            per = QROWS // block
            res[NT + j, pl.ds(i * per, per)] = (
                (mixed / total).astype(BF16).reshape(per, block, HDIM)
            )
            return inner

        return lax.fori_loop(0, tokens // QROWS, rows_step, carry)

    lax.fori_loop(0, NS, spatial, 0)

    for j in range(NT):
        wait_bytes(res.at[j, pl.ds(0, frames - 1)], ret_recv.at[j])
    for h in range(heads):
        total = None
        for slot in range(NT + NS):
            if fits(slot, h):
                term = res[slot].reshape(tokens, HDIM) * one_hot[slot, h]
                total = term if total is None else total + term
        out_ref[:, h * HDIM : (h + 1) * HDIM] = total

    wait_bytes(ss_all.at[pl.ds(0, groups - 1)], ss_sems.at[0])
    for j in range(NT):
        wait_bytes(vt.at[j, pl.ds(0, frames - 1)], vt_send.at[j])
        wait_bytes(qkt.at[j, :, pl.ds(0, frames - 1)], qk_send.at[j])
        wait_bytes(ot.at[j, pl.ds(0, frames - 1)], ret_send.at[j])
    for j in range(NS):
        pair_copy(own_k, par_k, sk_send, sk_recv, j).wait_send()
        pair_copy(own_v, par_v, sv_send, sv_recv, j).wait_send()


def shards(query, key, value, gain_q, gain_k, head_kind):
    tokens, width = query.shape
    frames = lax.axis_size("ctx") // 2
    groups = lax.axis_size("head")
    block = tokens // frames
    vmem = pl.BlockSpec(memory_space=pltpu.VMEM)
    dma = pltpu.SemaphoreType.DMA
    return pl.pallas_call(
        functools.partial(kernel, frames, groups),
        out_shape=jax.ShapeDtypeStruct((tokens, width), BF16),
        in_specs=[pl.BlockSpec(memory_space=pltpu.SMEM)] + [vmem] * 5,
        out_specs=vmem,
        scratch_shapes=[
            pltpu.VMEM((NT, frames, block, HDIM), BF16),
            pltpu.VMEM((NT, 2, frames, block, HDIM), BF16),
            pltpu.VMEM((NT, frames, block, HDIM), BF16),
            pltpu.VMEM((NT, 2, frames, block, HDIM), BF16),
            pltpu.VMEM((NT, frames, block, HDIM), BF16),
            pltpu.VMEM((NT + NS, frames, block, HDIM), BF16),
            pltpu.VMEM((NS, tokens, HDIM), BF16),
            pltpu.VMEM((NS, tokens, HDIM), BF16),
            pltpu.VMEM((NS, tokens, HDIM), BF16),
            pltpu.VMEM((NS, tokens, HDIM), BF16),
            pltpu.VMEM((NS, tokens, HDIM), BF16),
            pltpu.VMEM((tokens, width), BF16),
            pltpu.VMEM((tokens, width), BF16),
            pltpu.VMEM((tokens, HDIM), F32),
            pltpu.VMEM((tokens, HDIM), F32),
            pltpu.VMEM((2, 8, CHUNK), F32),
            pltpu.VMEM((groups, 2, 8, CHUNK), F32),
            dma((2,)),
            dma((NT,)), dma((NT,)), dma((NT,)), dma((NT,)), dma((NT,)), dma((NT,)),
            dma((NS,)), dma((NS,)), dma((NS,)), dma((NS,)),
        ],
        compiler_params=pltpu.CompilerParams(
            collective_id=0, has_side_effects=True, vmem_limit_bytes=56 * 2**20
        ),
        cost_estimate=pl.CostEstimate(
            flops=4 * NS * tokens * 2 * tokens * HDIM,
            bytes_accessed=8 * tokens * width,
            transcendentals=NS * 2 * tokens * tokens,
        ),
        name="head_attention",
    )(head_kind, query, key, value, gain_q.reshape(1, -1), gain_k.reshape(1, -1))


def solution(mesh):
    return jax.shard_map(
        shards,
        mesh=mesh,
        in_specs=(P("ctx", "head"), P("ctx", "head"), P("ctx", "head"), P("head"), P("head"), P()),
        out_specs=P("ctx", "head"),
        check_vma=False,
    )
```

time: 315 us -> 133 us (0.42); the launches traced: 310 us -> 133 us
  waiting for transfers between devices: 173 us -> 0 us
  Pallas kernels: 0 us -> 128 us
  matrix products: 39.3 us -> 0 us
  starting transfers between devices: 33.3 us -> 0 us
  other arithmetic: 23.8 us -> 0 us
  local copies, waits for them, and re-layouts: 22.7 us -> 5.01 us
  blocking collectives: 15.2 us -> 0 us
  loops' own time: 3.18 us -> 0 us
    pallas_call x0 -> x1, Pallas kernels: none -> 128 us  [shards(): pl.pallas_call(functools.partial(kernel, frames, groups), out_shape=jax.S...]
    ppermute x2 -> x0, waiting for transfers between devices: 88.3 us -> none  [partner(): lax.ppermute(shard, axis, [(i, i ^ 1 << distance) for i in range(lax.axis...]
    all_to_all x4 -> x0, waiting for transfers between devices: 84.2 us -> none  [the longest x1 43.6 us: shards(): lax.all_to_all(outgoing[1], 'ctx', split_axis=1, concat_axis=0, tiled=True)]
    dot_general x12 -> x0, matrix products: 39.3 us -> none  [the longest x5 19.6 us: spatial_head(): jnp.einsum('ps,sd->pd', weights, value_head, preferred_element_type=jnp.f...]
    all_to_all x4 -> x0, starting transfers between devices: 30.8 us -> none  [the longest x1 9.73 us: shards(): lax.all_to_all(outgoing[1], 'ctx', split_axis=1, concat_axis=0, tiled=True)]
    psum x1 -> x0, blocking collectives: 15.2 us -> none  [shards(): lax.psum((jnp.sum(query_float * query_float, axis=1), jnp.sum(key_float *...]
    reduce_sum x6 -> x0, other arithmetic: 10.3 us -> none  [the longest x5 9.67 us: softmax_weights(): jnp.sum(expo_terms, axis=-1, keepdims=True)]
    another operation x3 -> x0, local copies, waits for them, and re-layouts: 9.59 us -> none  [shards(): outgoing = (query_three[None], key_three[None], value_three[None])]
  transfers between devices with their start and end apart: 6 -> 0, of which waited for: 4 -> 0; matrix products, arithmetic and copies ran while one was open for 22% -> 0% of each run, Pallas kernels for 0% -> 0%
where the time goes in v1:
time: 133 us
  Pallas kernels  128 us (96%)
  local copies, waits for them, and re-layouts  5.01 us (4%)
    pallas_call x1, Pallas kernels, shards(): pl.pallas_call(functools.partial(kernel, frames, groups), out_shape=jax.S...  128 us

profile of v1, /device:TPU:1, one launch (start us, length us, event | category | flops | bytes accessed | tf_op | source)
XLA Modules:
  0.0 133.1 jit_solution(2438500228149786440)
XLA Ops:
  0.0 1.3 reshape.6.gq_ref
  1.3 1.3 reshape.7.gk_ref
  2.5 128.1 %head_attention.1 = bf16[1024,640]{1,0:T(8,128)(2,1)} custom-call(s32[40]{0:T(128)} %kind_ref.1, bf16[1024,640]{1,0:T(8,128)(2,1)} %q_ref.1, bf16[1024,640]{1,0:T(8,128)(2,1)} %k_ref.1, bf16[1024,640]{1,0:T(8,128)(2,1)} %v_ref.1, f32[1,640]{1,0:T(1,128)} %reshape.6.gq_ref, f32[1,640]{1,0:T(1,128)} %reshape.7.gk_ref), custom_call_target="tpu_custom_call" | custom-call | flops 4294967296 | bytes 5242880 | tf_op jit(solution)/shard_map/head_attention/pallas_call | solution.py:278
  130.7 2.5 %copy.8 = bf16[1024,640]{1,0:T(8,128)(2,1)} copy(bf16[1024,640]{1,0:T(8,128)(2,1)} %head_attention.1) | data formatting | bytes 2621440

commit v2 on v1

v2 whole, which is shorter than its diff:
```python
import functools
import math

import jax
import jax.numpy as jnp
from jax import lax
from jax.experimental import pallas as pl
from jax.experimental.pallas import tpu as pltpu
from jax.sharding import PartitionSpec as P

HEADS = 40
HDIM = 128
EPSILON = 1e-06
NT = 3
NS = 4
ND = 2
FLEX = (2, 1)
SPATIAL_OF = {2: 2, 1: 3}
MZ = 4
PAD = 256
CHUNK = 128
QROWS = 256
MESH = pl.DeviceIdType.MESH
BF16 = jnp.bfloat16
F32 = jnp.float32


def dot_nt(a, b):
    return lax.dot_general(a, b, (((1,), (1,)), ((), ())), preferred_element_type=F32)


def dot_nn(a, b):
    return lax.dot_general(a, b, (((1,), (0,)), ((), ())), preferred_element_type=F32)


def kernel(
    frames, groups, kind_ref, q_ref, k_ref, v_ref, gq_ref, gk_ref, out_ref,
    snd, rcv, ot, res, own, par, qs, qn, kn, rq, rk, ss_own, ss_all, out_msg, near_msg, far_msg,
    ss_sems, va_sems, qka_sems, ret_send, ret_recv, k_sems, v_sems,
    near_sems, out_send, out_recv, far_sems, fwd_send, fwd_recv,
):
    tokens, width = q_ref.shape
    heads = width // HDIM
    block = tokens // frames
    chunks = tokens // CHUNK
    score_scale = 1.0 / math.sqrt(HDIM)
    ctx = lax.axis_index("ctx")
    group = lax.axis_index("head")
    frame, half = ctx // 2, ctx % 2
    y, m = frame // MZ, frame % MZ
    sign = 1 - 2 * half
    partner = ctx + 1 - 2 * half
    ny = frames // MZ

    def frame_at(dy, dm):
        return lax.rem(y + dy + ny, ny) * MZ + lax.rem(m + dm + MZ, MZ)

    def to_ctx(to_frame, to_half):
        return {"ctx": 2 * to_frame + to_half}

    in_frames = [frame_at(b, sign) for b in range(4)] + [frame_at(b, 2) for b in (0, 1)]
    out_frames = [frame_at(b, -sign) for b in range(4)] + [frame_at(b, 2) for b in (2, 3)]

    barrier = pltpu.get_barrier_semaphore()

    def greet(device_id):
        pl.semaphore_signal(barrier, inc=1, device_id=device_id, device_id_type=MESH)

    def peer_of(d):
        return lax.rem(frame + d, frames)

    def greet_ctx(d, carry):
        greet(to_ctx(peer_of(d), half))
        return carry

    def greet_head(d, carry):
        greet({"head": lax.rem(group + d, groups)})
        return carry

    greet({"ctx": partner})
    for b in range(4):
        greet(to_ctx(frame_at(b, -sign), 1 - half))
    for b in (0, 1, 3):
        greet(to_ctx(frame_at(b, 2), 1 - half))
    lax.fori_loop(1, frames, greet_ctx, 0)
    lax.fori_loop(1, groups, greet_head, 0)

    one_hot = {}
    seen = jnp.zeros((1, HDIM), jnp.int32)
    for h in range(heads):
        kind = jnp.full((1, HDIM), kind_ref[group * heads + h], jnp.int32)
        for slot in range(NT + NS):
            if slot < NT:
                chosen = (kind == 1) & (seen == slot)
            else:
                chosen = (kind == 0) & (h - seen == slot - NT)
            one_hot[slot, h] = jnp.where(chosen, 1.0, 0.0).astype(BF16)
        seen = seen + kind

    def fits(slot, h):
        if slot < NT:
            return h >= slot
        return 0 <= h - (slot - NT) <= NT

    def pick(ref, slot):
        total = None
        for h in range(heads):
            if fits(slot, h):
                term = ref[:, h * HDIM : (h + 1) * HDIM] * one_hot[slot, h]
                total = term if total is None else total + term
        return total

    V, Q, K = (pl.ds(n * block, block) for n in range(3))
    KEYS, VALUES = pl.ds(0, tokens), pl.ds(tokens, tokens)

    def blocks_of(x):
        return x.reshape(frames, block, HDIM)

    def remote(src, dst, send, recv, device_id):
        return pltpu.make_async_remote_copy(
            src_ref=src, dst_ref=dst, send_sem=send, recv_sem=recv,
            device_id=device_id, device_id_type=MESH,
        )

    def wait_bytes(ref, sem):
        pltpu.make_async_copy(ref, ref, sem).wait()

    def pair_keys(j):
        return remote(own.at[j, KEYS], par.at[j, KEYS], k_sems.at[0, j], k_sems.at[1, j], {"ctx": partner})

    def pair_values(j):
        return remote(own.at[j, VALUES], par.at[j, VALUES], v_sems.at[0, j], v_sems.at[1, j], {"ctx": partner})

    snd[0, :, V, :] = blocks_of(pick(v_ref, 0))

    pl.semaphore_wait(barrier, frames - 1 + groups - 1 + 8)

    def send_va(d, carry):
        to = peer_of(d)
        remote(
            snd.at[0, to, V], rcv.at[0, frame, V], va_sems.at[0], va_sems.at[1], to_ctx(to, half)
        ).start()
        return carry

    lax.fori_loop(1, frames, send_va, 0)
    for j in range(ND):
        own[j, VALUES, :] = pick(v_ref, NT + j)
        pair_values(j).start()

    sub = lax.broadcasted_iota(jnp.int32, (8, CHUNK), 0)

    def squares(i, carry):
        rows = pl.ds(pl.multiple_of(i * CHUNK, CHUNK), CHUNK)
        kept = []
        for ref, tile in ((q_ref, carry[0]), (k_ref, carry[1])):
            part = ref[rows, :].astype(F32)
            total = jnp.sum(part * part, axis=1, keepdims=True)
            row = jnp.broadcast_to(total, (CHUNK, CHUNK)).T[0:8]
            kept.append(jnp.where(sub == i, row, tile))
        return tuple(kept)

    zero = jnp.zeros((8, CHUNK), F32)
    tiles = lax.fori_loop(0, chunks, squares, (zero, zero))
    for n in range(2):
        ss_own[n] = tiles[n]
        ss_all[group, n] = tiles[n]

    def send_squares(d, carry):
        remote(
            ss_own, ss_all.at[group], ss_sems.at[0], ss_sems.at[1],
            {"head": lax.rem(group + d, groups)},
        ).start()
        return carry

    lax.fori_loop(1, groups, send_squares, 0)

    for j in FLEX:
        snd[j, :, V, :] = blocks_of(pick(v_ref, j))
        own[SPATIAL_OF[j], VALUES, :] = pick(v_ref, NT + SPATIAL_OF[j])
        own[SPATIAL_OF[j], pl.ds(2 * tokens, PAD), :] = jnp.zeros((PAD, HDIM), BF16)

    wait_bytes(ss_all.at[pl.ds(0, groups - 1)], ss_sems.at[1])
    for n, column in ((0, rq), (1, rk)):
        total = ss_all[0, n]
        for g in range(1, groups):
            total = total + ss_all[g, n]
        inverse = lax.rsqrt(total * (1.0 / (HEADS * HDIM)) + EPSILON)
        for i in range(chunks):
            column[pl.ds(i * CHUNK, CHUNK), :] = jnp.broadcast_to(
                inverse[i : i + 1, :], (CHUNK, CHUNK)
            ).T

    for h in range(heads):
        at = slice(h * HDIM, (h + 1) * HDIM)
        qn[:, at] = (q_ref[:, at].astype(F32) * rq[...] * gq_ref[:, at]).astype(BF16)
        kn[:, at] = (k_ref[:, at].astype(F32) * rk[...] * gk_ref[:, at]).astype(BF16)

    size = 3 * block

    def near_copy(j):
        s = SPATIAL_OF[j]
        return remote(
            near_msg.at[j - 1], par.at[s, pl.ds(0, 6 * size)],
            near_sems.at[0, j - 1], near_sems.at[1, j - 1], {"ctx": partner},
        )

    def far_copy(j):
        s = SPATIAL_OF[j]
        return remote(
            far_msg.at[j - 1], par.at[s, pl.ds(6 * size, 6 * size)],
            far_sems.at[0, j - 1], far_sems.at[1, j - 1], {"ctx": partner},
        )

    for j in FLEX:
        s = SPATIAL_OF[j]
        snd[j, :, Q, :] = blocks_of(pick(qn, j))
        snd[j, :, K, :] = blocks_of(pick(kn, j))
        for b in range(6):
            remote(
                snd.at[j, out_frames[b]], out_msg.at[j - 1, pl.ds(b * size, size)],
                out_send.at[j - 1], out_recv.at[j - 1], to_ctx(frame_at(0, -sign), 1 - half),
            ).start()
        own[s, KEYS, :] = pick(kn, NT + s)
        for b in range(6):
            near_msg[j - 1, pl.ds(b * size, size), :] = (
                snd[j, in_frames[b]] + own[s, pl.ds(b * size, size), :]
            )
        near_copy(j).start()
        for b in range(1, 4):
            remote(
                snd.at[j, frame_at(b, 0)], rcv.at[j, frame],
                fwd_send.at[j - 1], fwd_recv.at[j - 1], to_ctx(frame_at(b, 0), half),
            ).start()
        rcv[j, frame] = snd[j, frame]
        qs[s] = pick(qn, NT + s)

    snd[0, :, Q, :] = blocks_of(pick(qn, 0))
    snd[0, :, K, :] = blocks_of(pick(kn, 0))
    QK = pl.ds(block, 2 * block)

    def send_qka(d, carry):
        to = peer_of(d)
        remote(
            snd.at[0, to, QK], rcv.at[0, frame, QK], qka_sems.at[0], qka_sems.at[1], to_ctx(to, half)
        ).start()
        return carry

    lax.fori_loop(1, frames, send_qka, 0)
    rcv[0, frame] = snd[0, frame]

    for j in FLEX:
        s = SPATIAL_OF[j]
        wait_bytes(out_msg.at[j - 1], out_recv.at[j - 1])
        for b in range(6):
            at = pl.ds(b * size, size)
            far_msg[j - 1, at, :] = out_msg[j - 1, at, :] + own[s, pl.ds((6 + b) * size, size), :]
        far_copy(j).start()

    for j in range(ND):
        own[j, KEYS, :] = pick(kn, NT + j)
        pair_keys(j).start()
        qs[j] = pick(qn, NT + j)

    for j in FLEX:
        s = SPATIAL_OF[j]
        near_copy(j).wait_recv()
        for b in range(6):
            to = frame_at(b, -sign) if b < 4 else frame_at(b - 4, 2)
            remote(
                par.at[s, pl.ds(b * size, size)], rcv.at[j, frame],
                fwd_send.at[j - 1], fwd_recv.at[j - 1], to_ctx(to, 1 - half),
            ).start()
    for j in FLEX:
        s = SPATIAL_OF[j]
        far_copy(j).wait_recv()
        origin = frame_at(0, sign)
        for b in range(1, 6):
            to = frame_at(b, 0) if b < 4 else frame_at(b - 2, -sign)
            remote(
                par.at[s, pl.ds((6 + b) * size, size)], rcv.at[j, origin],
                fwd_send.at[j - 1], fwd_recv.at[j - 1], to_ctx(to, half),
            ).start()
        rcv[j, origin] = par[s, pl.ds(6 * size, size), :]

    step_rows = 16 * frames
    same = (
        lax.rem(lax.broadcasted_iota(jnp.int32, (step_rows, step_rows), 0), 16)
        == lax.rem(lax.broadcasted_iota(jnp.int32, (step_rows, step_rows), 1), 16)
    )

    def temporal(j):
        def rows(n, c):
            return rcv[j, :, pl.ds(n * block + c * 16, 16), :].reshape(step_rows, HDIM)

        for c in range(block // 16):
            value, query, key = rows(0, c), rows(1, c), rows(2, c)
            scores = jnp.where(same, dot_nt(query, key) * score_scale, -jnp.inf)
            expo = jnp.exp(scores - jnp.max(scores, axis=1, keepdims=True))
            weights = (expo / jnp.sum(expo, axis=1, keepdims=True)).astype(BF16)
            mixed = dot_nn(weights, value).astype(BF16)
            ot[j, :, pl.ds(c * 16, 16), :] = mixed.reshape(frames, 16, HDIM)

        def send_ret(d, carry):
            to = peer_of(d)
            remote(
                ot.at[j, to], res.at[j, frame], ret_send.at[j], ret_recv.at[j], to_ctx(to, half)
            ).start()
            return carry

        lax.fori_loop(1, frames, send_ret, 0)
        res[j, frame] = ot[j, frame]

    def spatial(j):
        own_key, own_value, par_key, par_value = own[j, KEYS], own[j, VALUES], par[j, KEYS], par[j, VALUES]

        def rows_step(i, inner):
            query = qs[j, pl.ds(pl.multiple_of(i * QROWS, QROWS), QROWS), :]
            s_own = dot_nt(query, own_key) * score_scale
            s_par = dot_nt(query, par_key) * score_scale
            top = jnp.maximum(
                jnp.max(s_own, axis=1, keepdims=True), jnp.max(s_par, axis=1, keepdims=True)
            )
            e_own = jnp.exp(s_own - top)
            e_par = jnp.exp(s_par - top)
            total = jnp.sum(e_own, axis=1, keepdims=True) + jnp.sum(e_par, axis=1, keepdims=True)
            mixed = dot_nn(e_own.astype(BF16), own_value) + dot_nn(e_par.astype(BF16), par_value)
            per = QROWS // block
            res[NT + j, pl.ds(i * per, per)] = (
                (mixed / total).astype(BF16).reshape(per, block, HDIM)
            )
            return inner

        lax.fori_loop(0, tokens // QROWS, rows_step, 0)

    wait_bytes(rcv.at[0, pl.ds(0, frames - 1), V], va_sems.at[1])
    wait_bytes(rcv.at[0, pl.ds(0, frames - 1), QK], qka_sems.at[1])
    temporal(0)
    for j in FLEX:
        wait_bytes(rcv.at[j, pl.ds(0, frames - 2)], fwd_recv.at[j - 1])
        temporal(j)

    for j in range(ND):
        pair_values(j).wait_recv()
        pair_keys(j).wait_recv()

    def spatial_step(j, carry):
        spatial(j)
        return carry

    lax.fori_loop(0, NS, spatial_step, 0)

    for j in range(NT):
        wait_bytes(res.at[j, pl.ds(0, frames - 1)], ret_recv.at[j])
    for h in range(heads):
        total = None
        for slot in range(NT + NS):
            if fits(slot, h):
                term = res[slot].reshape(tokens, HDIM) * one_hot[slot, h]
                total = term if total is None else total + term
        out_ref[:, h * HDIM : (h + 1) * HDIM] = total

    wait_bytes(ss_all.at[pl.ds(0, groups - 1)], ss_sems.at[0])
    wait_bytes(snd.at[0, pl.ds(0, frames - 1), V], va_sems.at[0])
    wait_bytes(snd.at[0, pl.ds(0, frames - 1), QK], qka_sems.at[0])
    for j in range(NT):
        wait_bytes(ot.at[j, pl.ds(0, frames - 1)], ret_send.at[j])
    for j in FLEX:
        wait_bytes(out_msg.at[j - 1], out_send.at[j - 1])
        near_copy(j).wait_send()
        far_copy(j).wait_send()
        wait_bytes(rcv.at[j, pl.ds(0, frames - 2)], fwd_send.at[j - 1])
    for j in range(ND):
        pair_keys(j).wait_send()
        pair_values(j).wait_send()


def shards(query, key, value, gain_q, gain_k, head_kind):
    tokens, width = query.shape
    frames = lax.axis_size("ctx") // 2
    groups = lax.axis_size("head")
    block = tokens // frames
    vmem = pl.BlockSpec(memory_space=pltpu.VMEM)
    dma = pltpu.SemaphoreType.DMA
    return pl.pallas_call(
        functools.partial(kernel, frames, groups),
        out_shape=jax.ShapeDtypeStruct((tokens, width), BF16),
        in_specs=[pl.BlockSpec(memory_space=pltpu.SMEM)] + [vmem] * 5,
        out_specs=vmem,
        scratch_shapes=[
            pltpu.VMEM((NT, frames, 3 * block, HDIM), BF16),
            pltpu.VMEM((NT, frames, 3 * block, HDIM), BF16),
            pltpu.VMEM((NT, frames, block, HDIM), BF16),
            pltpu.VMEM((NT + NS, frames, block, HDIM), BF16),
            pltpu.VMEM((NS, 2 * tokens + PAD, HDIM), BF16),
            pltpu.VMEM((NS, 2 * tokens + PAD, HDIM), BF16),
            pltpu.VMEM((NS, tokens, HDIM), BF16),
            pltpu.VMEM((tokens, width), BF16),
            pltpu.VMEM((tokens, width), BF16),
            pltpu.VMEM((tokens, HDIM), F32),
            pltpu.VMEM((tokens, HDIM), F32),
            pltpu.VMEM((2, 8, CHUNK), F32),
            pltpu.VMEM((groups, 2, 8, CHUNK), F32),
            pltpu.VMEM((2, 18 * block, HDIM), BF16),
            pltpu.VMEM((2, 18 * block, HDIM), BF16),
            pltpu.VMEM((2, 18 * block, HDIM), BF16),
            dma((2,)), dma((2,)), dma((2,)), dma((NT,)), dma((NT,)), dma((2, ND)), dma((2, ND)),
            dma((2, 2)), dma((2,)), dma((2,)), dma((2, 2)), dma((2,)), dma((2,)),
        ],
        compiler_params=pltpu.CompilerParams(
            collective_id=0, has_side_effects=True, vmem_limit_bytes=56 * 2**20
        ),
        cost_estimate=pl.CostEstimate(
            flops=4 * NS * tokens * 2 * tokens * HDIM,
            bytes_accessed=8 * tokens * width,
            transcendentals=NS * 2 * tokens * tokens,
        ),
        name="head_attention",
    )(head_kind, query, key, value, gain_q.reshape(1, -1), gain_k.reshape(1, -1))


def solution(mesh):
    return jax.shard_map(
        shards,
        mesh=mesh,
        in_specs=(P("ctx", "head"), P("ctx", "head"), P("ctx", "head"), P("head"), P("head"), P()),
        out_specs=P("ctx", "head"),
        check_vma=False,
    )
```

time: 133 us -> 118 us (0.89)
  Pallas kernels: 128 us -> 113 us
    pallas_call x1, Pallas kernels: 128 us -> 113 us  [shards(): pl.pallas_call(functools.partial(kernel, frames, groups), out_shape=jax.S...]
where the time goes in v2:
time: 118 us
  Pallas kernels  113 us (96%)
  local copies, waits for them, and re-layouts  5.01 us (4%)
    pallas_call x1, Pallas kernels, shards(): pl.pallas_call(functools.partial(kernel, frames, groups), out_shape=jax.S...  113 us
    unnamed x1, local copies, waits for them, and re-layouts  2.49 us

profile of v2, /device:TPU:1, one launch (start us, length us, event | category | flops | bytes accessed | tf_op | source)
XLA Modules:
  0.0 117.6 jit_solution(14170646411884892094)
XLA Ops:
  0.0 1.3 %reshape.6.gq_ref = f32[1,640]{1,0:T(1,128)} reshape(f32[640]{0:T(1024)} %param.9) | data formatting | bytes 5120 | tf_op jit(solution)/shard_map/reshape | solution.py:418
  1.3 1.3 %reshape.7.gk_ref = f32[1,640]{1,0:T(1,128)} reshape(f32[640]{0:T(1024)} %param.10) | data formatting | bytes 5120 | tf_op jit(solution)/shard_map/reshape | solution.py:418
  2.5 112.6 %head_attention.1 = bf16[1024,640]{1,0:T(8,128)(2,1)} custom-call(s32[40]{0:T(128)} %kind_ref.1, bf16[1024,640]{1,0:T(8,128)(2,1)} %q_ref.1, bf16[1024,640]{1,0:T(8,128)(2,1)} %k_ref.1, bf16[1024,640]{1,0:T(8,128)(2,1)} %v_ref.1, f32[1,640]{1,0:T(1,128)} %reshape.6.gq_ref, f32[1,640]{1,0:T(1,128)} %reshape.7.gk_ref), custom_call_target="tpu_custom_call" | custom-call | flops 4294967296 | bytes 5242880 | tf_op jit(solution)/shard_map/head_attention/pallas_call | solution.py:384
  115.1 2.5 %copy.8 = bf16[1024,640]{1,0:T(8,128)(2,1)} copy(bf16[1024,640]{1,0:T(8,128)(2,1)} %head_attention.1) | data formatting | bytes 2621440

commit v3 on v2

--- a/solution.py
+++ b/solution.py
@@ -143,7 +143,7 @@
         return carry
 
     lax.fori_loop(1, frames, send_va, 0)
-    for j in range(ND):
+    for j in (0,):
         own[j, VALUES, :] = pick(v_ref, NT + j)
         pair_values(j).start()
 
@@ -192,8 +192,8 @@
 
     for h in range(heads):
         at = slice(h * HDIM, (h + 1) * HDIM)
-        qn[:, at] = (q_ref[:, at].astype(F32) * rq[...] * gq_ref[:, at]).astype(BF16)
-        kn[:, at] = (k_ref[:, at].astype(F32) * rk[...] * gk_ref[:, at]).astype(BF16)
+        qn[:, at] = (q_ref[:, at].astype(F32) * rq[...] * gq_ref[at]).astype(BF16)
+        kn[:, at] = (k_ref[:, at].astype(F32) * rk[...] * gk_ref[at]).astype(BF16)
 
     size = 3 * block
 
@@ -234,19 +234,10 @@
         rcv[j, frame] = snd[j, frame]
         qs[s] = pick(qn, NT + s)
 
-    snd[0, :, Q, :] = blocks_of(pick(qn, 0))
-    snd[0, :, K, :] = blocks_of(pick(kn, 0))
-    QK = pl.ds(block, 2 * block)
-
-    def send_qka(d, carry):
-        to = peer_of(d)
-        remote(
-            snd.at[0, to, QK], rcv.at[0, frame, QK], qka_sems.at[0], qka_sems.at[1], to_ctx(to, half)
-        ).start()
-        return carry
-
-    lax.fori_loop(1, frames, send_qka, 0)
-    rcv[0, frame] = snd[0, frame]
+    for j in (0,):
+        own[j, KEYS, :] = pick(kn, NT + j)
+        pair_keys(j).start()
+        qs[j] = pick(qn, NT + j)
 
     for j in FLEX:
         s = SPATIAL_OF[j]
@@ -255,11 +246,6 @@
             at = pl.ds(b * size, size)
             far_msg[j - 1, at, :] = out_msg[j - 1, at, :] + own[s, pl.ds((6 + b) * size, size), :]
         far_copy(j).start()
-
-    for j in range(ND):
-        own[j, KEYS, :] = pick(kn, NT + j)
-        pair_keys(j).start()
-        qs[j] = pick(qn, NT + j)
 
     for j in FLEX:
         s = SPATIAL_OF[j]
@@ -270,6 +256,9 @@
                 par.at[s, pl.ds(b * size, size)], rcv.at[j, frame],
                 fwd_send.at[j - 1], fwd_recv.at[j - 1], to_ctx(to, 1 - half),
             ).start()
+    for j in (1,):
+        own[j, VALUES, :] = pick(v_ref, NT + j)
+        pair_values(j).start()
     for j in FLEX:
         s = SPATIAL_OF[j]
         far_copy(j).wait_recv()
@@ -281,6 +270,25 @@
                 fwd_send.at[j - 1], fwd_recv.at[j - 1], to_ctx(to, half),
             ).start()
         rcv[j, origin] = par[s, pl.ds(6 * size, size), :]
+
+    snd[0, :, Q, :] = blocks_of(pick(qn, 0))
+    snd[0, :, K, :] = blocks_of(pick(kn, 0))
+    QK = pl.ds(block, 2 * block)
+
+    def send_qka(d, carry):
+        to = peer_of(d)
+        remote(
+            snd.at[0, to, QK], rcv.at[0, frame, QK], qka_sems.at[0], qka_sems.at[1], to_ctx(to, half)
+        ).start()
+        return carry
+
+    lax.fori_loop(1, frames, send_qka, 0)
+    rcv[0, frame] = snd[0, frame]
+
+    for j in (1,):
+        own[j, KEYS, :] = pick(kn, NT + j)
+        pair_keys(j).start()
+        qs[j] = pick(qn, NT + j)
 
     step_rows = 16 * frames
     same = (
@@ -332,22 +340,24 @@
 
         lax.fori_loop(0, tokens // QROWS, rows_step, 0)
 
+    def spatial_step(j, carry):
+        spatial(j)
+        return carry
+
+    pair_values(0).wait_recv()
+    pair_keys(0).wait_recv()
+    lax.fori_loop(0, 1, spatial_step, 0)
+    for j in FLEX:
+        wait_bytes(rcv.at[j, pl.ds(0, frames - 2)], fwd_recv.at[j - 1])
+        temporal(j)
+
     wait_bytes(rcv.at[0, pl.ds(0, frames - 1), V], va_sems.at[1])
     wait_bytes(rcv.at[0, pl.ds(0, frames - 1), QK], qka_sems.at[1])
     temporal(0)
-    for j in FLEX:
-        wait_bytes(rcv.at[j, pl.ds(0, frames - 2)], fwd_recv.at[j - 1])
-        temporal(j)
-
-    for j in range(ND):
-        pair_values(j).wait_recv()
-        pair_keys(j).wait_recv()
-
-    def spatial_step(j, carry):
-        spatial(j)
-        return carry
-
-    lax.fori_loop(0, NS, spatial_step, 0)
+    lax.fori_loop(ND, NS, spatial_step, 0)
+    pair_values(1).wait_recv()
+    pair_keys(1).wait_recv()
+    lax.fori_loop(1, 2, spatial_step, 0)
 
     for j in range(NT):
         wait_bytes(res.at[j, pl.ds(0, frames - 1)], ret_recv.at[j])
@@ -415,7 +425,7 @@
             transcendentals=NS * 2 * tokens * tokens,
         ),
         name="head_attention",
-    )(head_kind, query, key, value, gain_q.reshape(1, -1), gain_k.reshape(1, -1))
+    )(head_kind, query, key, value, gain_q, gain_k)
 
 
 def solution(mesh):

time: 118 us -> 108 us (0.915)
  Pallas kernels: 113 us -> 106 us
  local copies, waits for them, and re-layouts: 5.01 us -> 2.49 us
    pallas_call x1, Pallas kernels: 113 us -> 106 us  [shards(): pl.pallas_call(functools.partial(kernel, frames, groups), out_shape=jax.S...]
    reshape x2 -> x0, local copies, waits for them, and re-layouts: 2.53 us -> none  [the longest x1 1.27 us: shards(): gain_q.reshape(1, -1)]
where the time goes in v3:
time: 108 us
  Pallas kernels  106 us (98%)
  local copies, waits for them, and re-layouts  2.49 us (2%)
    pallas_call x1, Pallas kernels, shards(): pl.pallas_call(functools.partial(kernel, frames, groups), out_shape=jax.S...  106 us
    unnamed x1, local copies, waits for them, and re-layouts  2.49 us

profile of v3, /device:TPU:1, one launch (start us, length us, event | category | flops | bytes accessed | tf_op | source)
XLA Modules:
  0.0 108.2 jit_solution(5772584054791548699)
XLA Ops:
  0.0 105.7 %head_attention.1 = bf16[1024,640]{1,0:T(8,128)(2,1)} custom-call(s32[40]{0:T(128)} %kind_ref.1, bf16[1024,640]{1,0:T(8,128)(2,1)} %q_ref.1, bf16[1024,640]{1,0:T(8,128)(2,1)} %k_ref.1, bf16[1024,640]{1,0:T(8,128)(2,1)} %v_ref.1, f32[640]{0:T(1024)} %gq_ref.1, f32[640]{0:T(1024)} %gk_ref.1), custom_call_target="tpu_custom_call" | custom-call | flops 4294967296 | bytes 5242880 | tf_op jit(solution)/shard_map/head_attention/pallas_call | solution.py:394
  105.7 2.5 %copy.8 = bf16[1024,640]{1,0:T(8,128)(2,1)} copy(bf16[1024,640]{1,0:T(8,128)(2,1)} %head_attention.1) | data formatting | bytes 2621440

commit v4 on v3

--- a/solution.py
+++ b/solution.py
@@ -34,12 +34,12 @@
 
 
 def kernel(
-    frames, groups, kind_ref, q_ref, k_ref, v_ref, gq_ref, gk_ref, out_ref,
-    snd, rcv, ot, res, own, par, qs, qn, kn, rq, rk, ss_own, ss_all, out_msg, near_msg, far_msg,
+    frames, groups, kind_ref, q_hbm, k_hbm, v_hbm, gq_ref, gk_ref, res,
+    q_ref, k_ref, v_ref, load_sems, snd, rcv, ot, spat, own, par, qs, qn, kn, rq, rk, ss_own, ss_all, out_msg, near_msg, far_msg,
     ss_sems, va_sems, qka_sems, ret_send, ret_recv, k_sems, v_sems,
-    near_sems, out_send, out_recv, far_sems, fwd_send, fwd_recv,
+    near_sems, out_send, out_recv, far_sems, fwd_send, fwd_recv, self_sems, spat_sems,
 ):
-    tokens, width = q_ref.shape
+    tokens, width = q_hbm.shape
     heads = width // HDIM
     block = tokens // frames
     chunks = tokens // CHUNK
@@ -77,6 +77,13 @@
         greet({"head": lax.rem(group + d, groups)})
         return carry
 
+    loads = [
+        pltpu.make_async_copy(src, dst, load_sems.at[n])
+        for n, (src, dst) in enumerate(((v_hbm, v_ref), (q_hbm, q_ref), (k_hbm, k_ref)))
+    ]
+    for load in loads:
+        load.start()
+
     greet({"ctx": partner})
     for b in range(4):
         greet(to_ctx(frame_at(b, -sign), 1 - half))
@@ -131,6 +138,7 @@
     def pair_values(j):
         return remote(own.at[j, VALUES], par.at[j, VALUES], v_sems.at[0, j], v_sems.at[1, j], {"ctx": partner})
 
+    loads[0].wait()
     snd[0, :, V, :] = blocks_of(pick(v_ref, 0))
 
     pl.semaphore_wait(barrier, frames - 1 + groups - 1 + 8)
@@ -159,6 +167,8 @@
             kept.append(jnp.where(sub == i, row, tile))
         return tuple(kept)
 
+    loads[1].wait()
+    loads[2].wait()
     zero = jnp.zeros((8, CHUNK), F32)
     tiles = lax.fori_loop(0, chunks, squares, (zero, zero))
     for n in range(2):
@@ -316,7 +326,10 @@
             return carry
 
         lax.fori_loop(1, frames, send_ret, 0)
-        res[j, frame] = ot[j, frame]
+        pltpu.make_async_copy(ot.at[j, frame], res.at[j, frame], self_sems.at[j]).start()
+
+    def store_spatial(j):
+        return pltpu.make_async_copy(spat.at[j], res.at[NT + j], spat_sems.at[j])
 
     def spatial(j):
         own_key, own_value, par_key, par_value = own[j, KEYS], own[j, VALUES], par[j, KEYS], par[j, VALUES]
@@ -333,12 +346,13 @@
             total = jnp.sum(e_own, axis=1, keepdims=True) + jnp.sum(e_par, axis=1, keepdims=True)
             mixed = dot_nn(e_own.astype(BF16), own_value) + dot_nn(e_par.astype(BF16), par_value)
             per = QROWS // block
-            res[NT + j, pl.ds(i * per, per)] = (
+            spat[j, pl.ds(i * per, per)] = (
                 (mixed / total).astype(BF16).reshape(per, block, HDIM)
             )
             return inner
 
         lax.fori_loop(0, tokens // QROWS, rows_step, 0)
+        store_spatial(j).start()
 
     def spatial_step(j, carry):
         spatial(j)
@@ -361,14 +375,10 @@
 
     for j in range(NT):
         wait_bytes(res.at[j, pl.ds(0, frames - 1)], ret_recv.at[j])
-    for h in range(heads):
-        total = None
-        for slot in range(NT + NS):
-            if fits(slot, h):
-                term = res[slot].reshape(tokens, HDIM) * one_hot[slot, h]
-                total = term if total is None else total + term
-        out_ref[:, h * HDIM : (h + 1) * HDIM] = total
-
+    for j in range(NT):
+        pltpu.make_async_copy(ot.at[j, frame], res.at[j, frame], self_sems.at[j]).wait()
+    for j in range(NS):
+        store_spatial(j).wait()
     wait_bytes(ss_all.at[pl.ds(0, groups - 1)], ss_sems.at[0])
     wait_bytes(snd.at[0, pl.ds(0, frames - 1), V], va_sems.at[0])
     wait_bytes(snd.at[0, pl.ds(0, frames - 1), QK], qka_sems.at[0])
@@ -384,6 +394,27 @@
         pair_values(j).wait_send()
 
 
+def gather_heads(kind_ref, slots_ref, out_ref, held, sems):
+    heads = out_ref.shape[1] // HDIM
+    first = lax.axis_index("head") * heads
+    loads, stores = [], []
+    seen = jnp.int32(0)
+    for h in range(heads):
+        is_temporal = kind_ref[first + h] == 1
+        slot = jnp.where(is_temporal, seen, NT + h - seen)
+        seen = seen + kind_ref[first + h]
+        loads.append(pltpu.make_async_copy(slots_ref.at[slot], held.at[h], sems.at[0, h]))
+        stores.append(
+            pltpu.make_async_copy(held.at[h], out_ref.at[:, pl.ds(h * HDIM, HDIM)], sems.at[1, h])
+        )
+        loads[-1].start()
+    for load, store in zip(loads, stores):
+        load.wait()
+        store.start()
+    for store in stores:
+        store.wait()
+
+
 def shards(query, key, value, gain_q, gain_k, head_kind):
     tokens, width = query.shape
     frames = lax.axis_size("ctx") // 2
@@ -391,16 +422,20 @@
     block = tokens // frames
     vmem = pl.BlockSpec(memory_space=pltpu.VMEM)
     dma = pltpu.SemaphoreType.DMA
-    return pl.pallas_call(
+    slots = pl.pallas_call(
         functools.partial(kernel, frames, groups),
-        out_shape=jax.ShapeDtypeStruct((tokens, width), BF16),
-        in_specs=[pl.BlockSpec(memory_space=pltpu.SMEM)] + [vmem] * 5,
-        out_specs=vmem,
+        out_shape=jax.ShapeDtypeStruct((NT + NS, frames, block, HDIM), BF16),
+        in_specs=[pl.BlockSpec(memory_space=pltpu.SMEM)] + [pl.BlockSpec(memory_space=pl.ANY)] * 3 + [vmem] * 2,
+        out_specs=pl.BlockSpec(memory_space=pl.ANY),
         scratch_shapes=[
+            pltpu.VMEM((tokens, width), BF16),
+            pltpu.VMEM((tokens, width), BF16),
+            pltpu.VMEM((tokens, width), BF16),
+            dma((3,)),
             pltpu.VMEM((NT, frames, 3 * block, HDIM), BF16),
             pltpu.VMEM((NT, frames, 3 * block, HDIM), BF16),
             pltpu.VMEM((NT, frames, block, HDIM), BF16),
-            pltpu.VMEM((NT + NS, frames, block, HDIM), BF16),
+            pltpu.VMEM((NS, frames, block, HDIM), BF16),
             pltpu.VMEM((NS, 2 * tokens + PAD, HDIM), BF16),
             pltpu.VMEM((NS, 2 * tokens + PAD, HDIM), BF16),
             pltpu.VMEM((NS, tokens, HDIM), BF16),
@@ -414,7 +449,7 @@
             pltpu.VMEM((2, 18 * block, HDIM), BF16),
             pltpu.VMEM((2, 18 * block, HDIM), BF16),
             dma((2,)), dma((2,)), dma((2,)), dma((NT,)), dma((NT,)), dma((2, ND)), dma((2, ND)),
-            dma((2, 2)), dma((2,)), dma((2,)), dma((2, 2)), dma((2,)), dma((2,)),
+            dma((2, 2)), dma((2,)), dma((2,)), dma((2, 2)), dma((2,)), dma((2,)), dma((NT,)), dma((NS,)),
         ],
         compiler_params=pltpu.CompilerParams(
             collective_id=0, has_side_effects=True, vmem_limit_bytes=56 * 2**20
@@ -426,6 +461,14 @@
         ),
         name="head_attention",
     )(head_kind, query, key, value, gain_q, gain_k)
+    return pl.pallas_call(
+        gather_heads,
+        out_shape=jax.ShapeDtypeStruct((tokens, width), BF16),
+        in_specs=[pl.BlockSpec(memory_space=pltpu.SMEM), pl.BlockSpec(memory_space=pl.ANY)],
+        out_specs=pl.BlockSpec(memory_space=pl.ANY),
+        scratch_shapes=[pltpu.VMEM((width // HDIM, tokens, HDIM), BF16), dma((2, width // HDIM))],
+        name="gather_heads",
+    )(head_kind, slots.reshape(NT + NS, tokens, HDIM))
 
 
 def solution(mesh):

time: 108 us -> 106 us (0.981)
  local copies, waits for them, and re-layouts: 2.49 us -> 0 us
    pallas_call x1, Pallas kernels: 106 us -> 103 us  [shards(): pl.pallas_call(functools.partial(kernel, frames, groups), out_shape=jax.S...]
    pallas_call x0 -> x1, Pallas kernels: none -> 2.76 us  [shards(): pl.pallas_call(gather_heads, out_shape=jax.ShapeDtypeStruct((tokens, widt...]
    unnamed x1 -> x0, local copies, waits for them, and re-layouts: 2.49 us -> none
where the time goes in v4:
time: 106 us; the launch traced here: 105 us
  Pallas kernels  105 us (99%)
    pallas_call x1, Pallas kernels, shards(): pl.pallas_call(functools.partial(kernel, frames, groups), out_shape=jax.S...  103 us
    pallas_call x1, Pallas kernels, shards(): pl.pallas_call(gather_heads, out_shape=jax.ShapeDtypeStruct((tokens, widt...  2.76 us

profile of v4, /device:TPU:1, one launch (start us, length us, event | category | flops | bytes accessed | tf_op | source)
XLA Modules:
  0.0 105.4 jit_solution(3930010841129744287)
XLA Ops:
  0.0 102.7 %head_attention.1 = bf16[7,16,64,128]{3,2,1,0:T(8,128)(2,1)} custom-call(s32[40]{0:T(128)} %kind_ref.3, bf16[1024,640]{1,0:T(8,128)(2,1)} %q_hbm.1, bf16[1024,640]{1,0:T(8,128)(2,1)} %k_hbm.1, bf16[1024,640]{1,0:T(8,128)(2,1)} %v_hbm.1, f32[640]{0:T(1024)} %gq_ref.1, f32[640]{0:T(1024)} %gk_ref.1), custom_call_target="tpu_custom_call" | custom-call | flops 4294967296 | bytes 5242880 | tf_op jit(solution)/shard_map/head_attention/pallas_call | solution.py:425
  102.7 2.8 %gather_heads.1 = bf16[1024,640]{1,0:T(8,128)(2,1)} custom-call(s32[40]{0:T(128)} %kind_ref.3, bf16[7,1024,128]{2,1,0:T(8,128)(2,1)} %bitcast.1), custom_call_target="tpu_custom_call" | custom-call | tf_op jit(solution)/shard_map/gather_heads/pallas_call | solution.py:464

commit v5 on v4

--- a/solution.py
+++ b/solution.py
@@ -34,8 +34,8 @@
 
 
 def kernel(
-    frames, groups, kind_ref, q_hbm, k_hbm, v_hbm, gq_ref, gk_ref, res,
-    q_ref, k_ref, v_ref, load_sems, snd, rcv, ot, spat, own, par, qs, qn, kn, rq, rk, ss_own, ss_all, out_msg, near_msg, far_msg,
+    frames, groups, kind_hbm, q_hbm, k_hbm, v_hbm, gq_hbm, gk_hbm, res,
+    kind_ref, gq_ref, gk_ref, q_ref, k_ref, v_ref, load_sems, snd, rcv, ot, spat, own, par, qs, qn, kn, rq, rk, ss_own, ss_all, out_msg, near_msg, far_msg,
     ss_sems, va_sems, qka_sems, ret_send, ret_recv, k_sems, v_sems,
     near_sems, out_send, out_recv, far_sems, fwd_send, fwd_recv, self_sems, spat_sems,
 ):
@@ -79,10 +79,13 @@
 
     loads = [
         pltpu.make_async_copy(src, dst, load_sems.at[n])
-        for n, (src, dst) in enumerate(((v_hbm, v_ref), (q_hbm, q_ref), (k_hbm, k_ref)))
+        for n, (src, dst) in enumerate((
+            (v_hbm, v_ref), (q_hbm, q_ref), (k_hbm, k_ref),
+            (gq_hbm, gq_ref), (gk_hbm, gk_ref), (kind_hbm, kind_ref),
+        ))
     ]
-    for load in loads:
-        load.start()
+    for n in (5, 0, 1, 2, 3, 4):
+        loads[n].start()
 
     greet({"ctx": partner})
     for b in range(4):
@@ -92,6 +95,7 @@
     lax.fori_loop(1, frames, greet_ctx, 0)
     lax.fori_loop(1, groups, greet_head, 0)
 
+    loads[5].wait()
     one_hot = {}
     seen = jnp.zeros((1, HDIM), jnp.int32)
     for h in range(heads):
@@ -168,7 +172,8 @@
         return tuple(kept)
 
     loads[1].wait()
-    loads[2].wait()
+    for n in (2, 3, 4):
+        loads[n].wait()
     zero = jnp.zeros((8, CHUNK), F32)
     tiles = lax.fori_loop(0, chunks, squares, (zero, zero))
     for n in range(2):
@@ -361,13 +366,13 @@
     pair_values(0).wait_recv()
     pair_keys(0).wait_recv()
     lax.fori_loop(0, 1, spatial_step, 0)
-    for j in FLEX:
-        wait_bytes(rcv.at[j, pl.ds(0, frames - 2)], fwd_recv.at[j - 1])
-        temporal(j)
-
     wait_bytes(rcv.at[0, pl.ds(0, frames - 1), V], va_sems.at[1])
     wait_bytes(rcv.at[0, pl.ds(0, frames - 1), QK], qka_sems.at[1])
     temporal(0)
+    for j in FLEX:
+        wait_bytes(rcv.at[j, pl.ds(0, frames - 2)], fwd_recv.at[j - 1])
+        temporal(j)
+
     lax.fori_loop(ND, NS, spatial_step, 0)
     pair_values(1).wait_recv()
     pair_keys(1).wait_recv()
@@ -420,18 +425,20 @@
     frames = lax.axis_size("ctx") // 2
     groups = lax.axis_size("head")
     block = tokens // frames
-    vmem = pl.BlockSpec(memory_space=pltpu.VMEM)
     dma = pltpu.SemaphoreType.DMA
     slots = pl.pallas_call(
         functools.partial(kernel, frames, groups),
         out_shape=jax.ShapeDtypeStruct((NT + NS, frames, block, HDIM), BF16),
-        in_specs=[pl.BlockSpec(memory_space=pltpu.SMEM)] + [pl.BlockSpec(memory_space=pl.ANY)] * 3 + [vmem] * 2,
+        in_specs=[pl.BlockSpec(memory_space=pl.ANY)] * 6,
         out_specs=pl.BlockSpec(memory_space=pl.ANY),
         scratch_shapes=[
+            pltpu.SMEM(head_kind.shape, jnp.int32),
+            pltpu.VMEM((width,), F32),
+            pltpu.VMEM((width,), F32),
             pltpu.VMEM((tokens, width), BF16),
             pltpu.VMEM((tokens, width), BF16),
             pltpu.VMEM((tokens, width), BF16),
-            dma((3,)),
+            dma((6,)),
             pltpu.VMEM((NT, frames, 3 * block, HDIM), BF16),
             pltpu.VMEM((NT, frames, 3 * block, HDIM), BF16),
             pltpu.VMEM((NT, frames, block, HDIM), BF16),

time: 106 us -> 105 us (level)
  no operation moved by 1% of the time
where the time goes in v5:
time: 105 us
  Pallas kernels  105 us (100%)
    pallas_call x1, Pallas kernels, shards(): pl.pallas_call(functools.partial(kernel, frames, groups), out_shape=jax.S...  102 us
    pallas_call x1, Pallas kernels, shards(): pl.pallas_call(gather_heads, out_shape=jax.ShapeDtypeStruct((tokens, widt...  2.76 us

profile of v5, /device:TPU:1, one launch (start us, length us, event | category | flops | bytes accessed | tf_op | source)
XLA Modules:
  0.0 104.7 jit_solution(15960430984978051129)
XLA Ops:
  0.0 101.9 %head_attention.1 = bf16[7,16,64,128]{3,2,1,0:T(8,128)(2,1)} custom-call(s32[40]{0:T(128)} %kind_ref.1, bf16[1024,640]{1,0:T(8,128)(2,1)} %q_hbm.1, bf16[1024,640]{1,0:T(8,128)(2,1)} %k_hbm.1, bf16[1024,640]{1,0:T(8,128)(2,1)} %v_hbm.1, f32[640]{0:T(1024)} %gq_hbm.1, f32[640]{0:T(1024)} %gk_hbm.1), custom_call_target="tpu_custom_call" | custom-call | flops 4294967296 | bytes 5242880 | tf_op jit(solution)/shard_map/head_attention/pallas_call | solution.py:429
  101.9 2.8 %gather_heads.1 = bf16[1024,640]{1,0:T(8,128)(2,1)} custom-call(s32[40]{0:T(128)} %kind_ref.1, bf16[7,1024,128]{2,1,0:T(8,128)(2,1)} %bitcast.1), custom_call_target="tpu_custom_call" | custom-call | tf_op jit(solution)/shard_map/gather_heads/pallas_call | solution.py:471

commit v6 on v5

--- a/solution.py
+++ b/solution.py
@@ -399,22 +399,31 @@
         pair_values(j).wait_send()
 
 
-def gather_heads(kind_ref, slots_ref, out_ref, held, sems):
+def gather_heads(kind_hbm, slots_ref, out_ref, kind_ref, held, kind_sem, load_sems, store_sems):
     heads = out_ref.shape[1] // HDIM
     first = lax.axis_index("head") * heads
-    loads, stores = [], []
+    kinds = pltpu.make_async_copy(kind_hbm, kind_ref, kind_sem)
+    kinds.start()
+    loads = [
+        pltpu.make_async_copy(slots_ref.at[n], held.at[n], load_sems.at[n]) for n in range(NT + NS)
+    ]
+    for load in loads:
+        load.start()
+    kinds.wait()
+    stores = []
     seen = jnp.int32(0)
     for h in range(heads):
         is_temporal = kind_ref[first + h] == 1
         slot = jnp.where(is_temporal, seen, NT + h - seen)
         seen = seen + kind_ref[first + h]
-        loads.append(pltpu.make_async_copy(slots_ref.at[slot], held.at[h], sems.at[0, h]))
         stores.append(
-            pltpu.make_async_copy(held.at[h], out_ref.at[:, pl.ds(h * HDIM, HDIM)], sems.at[1, h])
+            pltpu.make_async_copy(
+                held.at[slot], out_ref.at[:, pl.ds(h * HDIM, HDIM)], store_sems.at[h]
+            )
         )
-        loads[-1].start()
-    for load, store in zip(loads, stores):
+    for load in loads:
         load.wait()
+    for store in stores:
         store.start()
     for store in stores:
         store.wait()
@@ -471,9 +480,13 @@
     return pl.pallas_call(
         gather_heads,
         out_shape=jax.ShapeDtypeStruct((tokens, width), BF16),
-        in_specs=[pl.BlockSpec(memory_space=pltpu.SMEM), pl.BlockSpec(memory_space=pl.ANY)],
+        in_specs=[pl.BlockSpec(memory_space=pl.ANY)] * 2,
         out_specs=pl.BlockSpec(memory_space=pl.ANY),
-        scratch_shapes=[pltpu.VMEM((width // HDIM, tokens, HDIM), BF16), dma((2, width // HDIM))],
+        scratch_shapes=[
+            pltpu.SMEM(head_kind.shape, jnp.int32),
+            pltpu.VMEM((NT + NS, tokens, HDIM), BF16),
+            dma, dma((NT + NS,)), dma((width // HDIM,)),
+        ],
         name="gather_heads",
     )(head_kind, slots.reshape(NT + NS, tokens, HDIM))
 

time: 105 us -> 105 us (level)
  no operation moved by 1% of the time
where the time goes in v6:
time: 105 us; the launch traced here: 104 us
  Pallas kernels  104 us (99%)
    pallas_call x1, Pallas kernels, shards(): pl.pallas_call(functools.partial(kernel, frames, groups), out_shape=jax.S...  102 us
    pallas_call x1, Pallas kernels, shards(): pl.pallas_call(gather_heads, out_shape=jax.ShapeDtypeStruct((tokens, widt...  2.58 us

profile of v6, /device:TPU:1, one launch (start us, length us, event | category | flops | bytes accessed | tf_op | source)
XLA Modules:
  0.0 104.5 jit_solution(778093810648843393)
XLA Ops:
  0.0 101.9 %head_attention.1 = bf16[7,16,64,128]{3,2,1,0:T(8,128)(2,1)} custom-call(s32[40]{0:T(128)} %kind_hbm.3, bf16[1024,640]{1,0:T(8,128)(2,1)} %q_hbm.1, bf16[1024,640]{1,0:T(8,128)(2,1)} %k_hbm.1, bf16[1024,640]{1,0:T(8,128)(2,1)} %v_hbm.1, f32[640]{0:T(1024)} %gq_hbm.1, f32[640]{0:T(1024)} %gk_hbm.1), custom_call_target="tpu_custom_call" | custom-call | flops 4294967296 | bytes 5242880 | tf_op jit(solution)/shard_map/head_attention/pallas_call | solution.py:438
  101.9 2.6 %gather_heads.1 = bf16[1024,640]{1,0:T(8,128)(2,1)} custom-call(s32[40]{0:T(128)} %kind_hbm.3, bf16[7,1024,128]{2,1,0:T(8,128)(2,1)} %bitcast.1), custom_call_target="tpu_custom_call" | custom-call | tf_op jit(solution)/shard_map/gather_heads/pallas_call | solution.py:480
